TPU v7x, 32 devices: a whole 2x2x4 slice. The times are simulated.
32 devices in a mesh: chan: 4 (over z), rows: 8 (over y, x, core).
Axes of the slice: x: 2, y: 2, z: 4, core: 2. Of those that a mesh axis runs over, the one named last changes fastest.
Arguments:
- tokens: bfloat16 [512, 512, 512], P('rows', None, 'chan'), may hold values from -60 to 60
- gain_in: float32 [512], P('chan'), may hold values from 0.1 to 1.9
- spectral_w1: float32 [2, 8, 64, 64], P(None, 'chan'), may hold values from -0.75 to 0.75
- spectral_b1: float32 [2, 8, 64], P(None, 'chan'), may hold values from -3 to 3
- spectral_w2: float32 [2, 8, 64, 64], P(None, 'chan'), may hold values from -0.75 to 0.75
- spectral_b2: float32 [2, 8, 64], P(None, 'chan'), may hold values from -3 to 3
- gain_out: float32 [512], replicated, may hold values from 0.1 to 1.9
- fc1_weight: bfloat16 [512, 2048], P(None, 'chan'), may hold values from -0.25 to 0.25
- fc1_bias: bfloat16 [2048], P('chan'), may hold values from -3 to 3
- fc2_weight: bfloat16 [2048, 512], P('chan'), may hold values from -0.1875 to 0.1875
- fc2_bias: bfloat16 [512], P('chan'), may hold values from -3 to 3
Outputs:
- block_out: bfloat16 [512, 512, 512], P('rows', None, 'chan')
All inputs are finite; a program needn't handle non-finite values.
Results may differ from a plain program's by a relative error of at most 0.0055.
Values may be sent and summed in bfloat16 or wider, within the bound.
A program may use at most 192 MiB of HBM per device.

v0:
```python
import math

import jax
import jax.numpy as jnp
from jax import lax
from jax.sharding import PartitionSpec as P

norm_eps = 1e-05
shrink_level = 0.01
highest = lax.Precision.HIGHEST


def normalize(values, gain):
    center = jnp.mean(values, axis=-1, keepdims=True)
    spread = jnp.mean(values * values, axis=-1, keepdims=True) - center * center
    return (values - center) * lax.rsqrt(spread + norm_eps) * gain


def soften(values):
    return jnp.where(
        values > shrink_level,
        values - shrink_level,
        jnp.where(values < -shrink_level, values + shrink_level, 0.0),
    )


def complex_sum(real_part, imag_part, table_cos, table_sin, form):
    first_cos = jnp.einsum(form, real_part, table_cos, precision=highest)
    first_sin = jnp.einsum(form, real_part, table_sin, precision=highest)
    second_cos = jnp.einsum(form, imag_part, table_cos, precision=highest)
    second_sin = jnp.einsum(form, imag_part, table_sin, precision=highest)
    return (first_cos - second_sin, first_sin + second_cos)


def column_transform(real_part, imag_part, sign):
    length = real_part.shape[0]
    trailing = real_part.shape[1:]
    outer_len = max((factor for factor in range(1, math.isqrt(length) + 1) if length % factor == 0))
    inner_len = length // outer_len
    real_part = real_part.reshape(outer_len, inner_len, -1)
    imag_part = imag_part.reshape(outer_len, inner_len, -1)
    outer_idx = jnp.arange(outer_len, dtype=jnp.int32)
    inner_idx = jnp.arange(inner_len, dtype=jnp.int32)
    angle = (
        2.0
        * math.pi
        / outer_len
        * (outer_idx[:, None] * outer_idx[None, :] % outer_len).astype(jnp.float32)
    )
    section_real, section_imag = complex_sum(
        real_part, imag_part, jnp.cos(angle), sign * jnp.sin(angle), "abm,ak->kbm"
    )
    twist = (
        2.0
        * math.pi
        / length
        * (outer_idx[:, None] * inner_idx[None, :] % length).astype(jnp.float32)
    )
    twist_cos = jnp.cos(twist)[:, :, None]
    twist_sin = sign * jnp.sin(twist)[:, :, None]
    section_real, section_imag = (
        section_real * twist_cos - section_imag * twist_sin,
        section_real * twist_sin + section_imag * twist_cos,
    )
    angle_two = (
        2.0
        * math.pi
        / inner_len
        * (inner_idx[:, None] * inner_idx[None, :] % inner_len).astype(jnp.float32)
    )
    final_real, final_imag = complex_sum(
        section_real, section_imag, jnp.cos(angle_two), sign * jnp.sin(angle_two), "kbm,bj->jkm"
    )
    scale = 1.0 / math.sqrt(length)
    return (
        final_real.reshape((length,) + trailing) * scale,
        final_imag.reshape((length,) + trailing) * scale,
    )


def block_matrix(weights):
    count = weights.shape[0]
    size = weights.shape[1]
    return jnp.einsum("nbo,nm->nbmo", weights, jnp.eye(count, dtype=weights.dtype)).reshape(
        count * size, count * size
    )


def spectral_layer(real_part, imag_part, weights, biases):
    weight_real = block_matrix(weights[0])
    weight_imag = block_matrix(weights[1])
    bias_real = biases[0].reshape(-1)
    bias_imag = biases[1].reshape(-1)
    real_out = (
        jnp.dot(real_part, weight_real, precision=highest)
        - jnp.dot(imag_part, weight_imag, precision=highest)
        + bias_real
    )
    imag_out = (
        jnp.dot(imag_part, weight_real, precision=highest)
        + jnp.dot(real_part, weight_imag, precision=highest)
        + bias_imag
    )
    return (real_out, imag_out)


def channel_mlp(token_rows, gain_out, first_weight, first_bias, second_weight):
    normed = normalize(token_rows.astype(jnp.float32), gain_out).astype(jnp.bfloat16)
    hidden = jax.nn.gelu(
        jnp.dot(normed, first_weight, preferred_element_type=jnp.float32)
        + first_bias.astype(jnp.float32),
        approximate=False,
    ).astype(jnp.bfloat16)
    return jnp.dot(hidden, second_weight, preferred_element_type=jnp.float32)


def local(
    tokens,
    gain_in,
    spectral_w1,
    spectral_b1,
    spectral_w2,
    spectral_b2,
    gain_out,
    fc1_weight,
    fc1_bias,
    fc2_weight,
    fc2_bias,
):
    row_count, grid_width, channels = tokens.shape
    chan_count = lax.axis_size("chan")
    all_channels = channels * chan_count
    source = tokens.astype(jnp.float32)
    totals, squares = lax.psum((jnp.sum(source, axis=2), jnp.sum(source * source, axis=2)), "chan")
    center = (totals / all_channels)[:, :, None]
    spread = (squares / all_channels)[:, :, None] - center * center
    normed = (source - center) * lax.rsqrt(spread + norm_eps) * gain_in
    half_width = grid_width // 2
    positions = jnp.arange(grid_width, dtype=jnp.int32)
    frequencies = jnp.arange(half_width, dtype=jnp.int32)
    row_scale = 1.0 / math.sqrt(grid_width)
    angle = (
        2.0
        * math.pi
        / grid_width
        * (positions[:, None] * frequencies[None, :] % grid_width).astype(jnp.float32)
    )
    forward_table = jnp.stack([jnp.cos(angle) * row_scale, -jnp.sin(angle) * row_scale])
    spectra = jnp.einsum("rwc,pwk->prkc", normed, forward_table, precision=highest)
    columns = lax.all_to_all(spectra, "rows", split_axis=2, concat_axis=1, tiled=True)
    col_real, col_imag = column_transform(columns[0], columns[1], -1.0)
    first_real, first_imag = spectral_layer(col_real, col_imag, spectral_w1, spectral_b1)
    second_real, second_imag = spectral_layer(
        jnp.maximum(first_real, 0.0), jnp.maximum(first_imag, 0.0), spectral_w2, spectral_b2
    )
    back_real, back_imag = column_transform(soften(second_real), soften(second_imag), 1.0)
    returned = lax.all_to_all(
        jnp.stack([back_real, back_imag]), "rows", split_axis=1, concat_axis=2, tiled=True
    )
    weighting = jnp.where(frequencies == 0, 1.0, 2.0).astype(jnp.float32) * row_scale
    inverse_table = jnp.stack(
        [jnp.cos(angle).T * weighting[:, None], -jnp.sin(angle).T * weighting[:, None]]
    )
    filtered = jnp.einsum("prkc,pkw->rwc", returned, inverse_table, precision=highest)
    mixed = (filtered + normed + source).astype(jnp.bfloat16)
    regrouped = lax.all_to_all(mixed, "chan", split_axis=1, concat_axis=2, tiled=True)
    first_full, bias_full = (
        lax.all_gather(fc1_weight, "chan", axis=1, tiled=True),
        lax.all_gather(fc1_bias[None, :], "chan", axis=1, tiled=True),
    )
    second_full = lax.all_gather(fc2_weight, "chan", axis=0, tiled=True)
    local_out = channel_mlp(
        regrouped.reshape(-1, all_channels), gain_out, first_full, bias_full[0], second_full
    )
    summed = lax.all_to_all(
        local_out.reshape(row_count, grid_width // chan_count, all_channels).astype(jnp.bfloat16),
        "chan",
        split_axis=2,
        concat_axis=1,
        tiled=True,
    ).astype(jnp.float32)
    return (mixed.astype(jnp.float32) + summed + fc2_bias.astype(jnp.float32)).astype(jnp.bfloat16)


def solution(mesh):
    return jax.shard_map(
        local,
        mesh=mesh,
        in_specs=(
            P("rows", None, "chan"),
            P("chan"),
            P(None, "chan", None, None),
            P(None, "chan", None),
            P(None, "chan", None, None),
            P(None, "chan", None),
            P(),
            P(None, "chan"),
            P("chan"),
            P("chan", None),
            P("chan"),
        ),
        out_specs=P("rows", None, "chan"),
        check_vma=False,
    )
```

profile of v0, /device:TPU:2, one launch (start us, length us, event | category | flops | bytes accessed | tf_op | source)
XLA Modules:
  0.0 1785.6 jit_solution(9867155288064247346)
XLA Ops:
  17.9 34.8 %all-reduce.3.cloned.1.call-done = (f32[64,512]{1,0:T(8,128)}, f32[64,512]{1,0:T(8,128)}) async-done(((f32[64,512]{1,0:T(8,128)}, f32[64,512]{1,0:T(8,128)}), (f32[64,512]{1,0:T(8,128)}, f32[64,512]{1,0:T(8,128)})) %all-reduce.3.cloned.1.call-update) | async-done | bytes 262160 | tf_op jit(solution)/shard_map/psum | solution.py:134
  54.5 34.3 %fusion.104 = f32[2,64,256,128]{3,2,1,0:T(8,128)S(1)} fusion(bf16[64,512,128]{2,1,0:T(8,128)(2,1)} %param.11, f32[128]{0:T(128)S(1)} %copy-done.17, f32[64,512]{1,0:T(8,128)S(1)} %get-tuple-element.22, f32[64,512]{1,0:T(8,128)S(1)} %get-tuple-element.21, f32[1,512,256]{1,2,0:T(8,128)S(1)} %get-tuple-element.33, f32[1,512,256]{1,2,0:T(8,128)S(1)} %get-tuple-element.34), kind=kOutput, calls=%fused_computation.110 | convolution fusion | flops 25786843136 | bytes 26477056 | tf_op jit(solution)/shard_map/rwc,pwk->prkc/dot_general | solution.py:149
  88.8 20.3 %copy.51 = f32[2,64,256,128]{3,1,0,2:T(8,128)} copy(f32[2,64,256,128]{3,2,1,0:T(8,128)S(1)} %fusion.104) | data formatting | bytes 33554432 | tf_op jit(solution)/shard_map/rwc,pwk->prkc/transpose | solution.py:149
  117.9 180.1 %all-to-all-done = f32[2,64,256,128]{3,1,0,2:T(8,128)} async-done(((f32[2,64,256,128]{3,1,0,2:T(8,128)}), f32[2,64,256,128]{3,1,0,2:T(8,128)}, u32[]{:S(2)}, u32[]{:S(2)}) %all-to-all-start) | async-done | bytes 16777248 | tf_op jit(solution)/shard_map/all_to_all | solution.py:150
  298.0 15.5 copy.169
  329.9 17.1 fusion.78
  369.4 18.2 %fusion.84 = f32[16,32,4096]{2,0,1:T(8,128)} fusion(f32[16,32,4096]{2,0,1:T(8,128)} %fusion.78, f32[16,32,4096]{2,1,0:T(8,128)} %reshape_squeeze.6), kind=kOutput, calls=%fused_computation.106 | convolution fusion | flops 404753920 | bytes 25165824 | tf_op jit(solution)/shard_map/abm,ak->kbm/dot_general | solution.py:28
  387.6 21.6 %multiply_subtract_fusion.1 = (f32[16,32,4096]{2,0,1:T(8,128)S(1)}, f32[16,32,4096]{2,0,1:T(8,128)}) fusion(f32[16,32,4096]{2,0,1:T(8,128)} %fusion.84, f32[16,32]{0,1:T(8,128)S(1)} %get-tuple-element.37, f32[16,32]{0,1:T(8,128)S(1)} %get-tuple-element.38, f32[16,32,4096]{2,0,1:T(8,128)} %fusion.76, f32[16,32,4096]{2,1,0:T(8,128)} %reshape_squeeze.6), kind=kOutput, calls=%fused_computation.62 | convolution fusion | flops 417337088 | bytes 41947136 | tf_op jit(solution)/shard_map/abm,ak->kbm/dot_general | solution.py:29
  409.2 18.0 %fusion.70 = f32[32,16,4096]{2,0,1:T(8,128)} fusion(f32[16,32,4096]{2,0,1:T(8,128)} %get-tuple-element.14), kind=kOutput, calls=%fused_computation.92 | convolution fusion | flops 805321728 | bytes 16777216 | tf_op jit(solution)/shard_map/kbm,bj->jkm/dot_general | solution.py:31
  439.9 15.9 subtract_multiply_fusion.1
  500.3 15.8 fusion.62
  529.8 16.3 add_maximum_fusion.1
  604.3 16.9 fusion.54
  660.8 18.1 %fusion.94 = f32[16,32,4096]{2,0,1:T(8,128)} fusion(f32[16,32,4096]{2,0,1:T(8,128)} %fusion.54, f32[16,32,4096]{2,1,0:T(8,128)} %reshape.362), kind=kOutput, calls=%fused_computation.108 | convolution fusion | flops 404753920 | bytes 25165824 | tf_op jit(solution)/shard_map/abm,ak->kbm/dot_general | solution.py:28
  678.9 22.0 %multiply_subtract_fusion = (f32[16,32,4096]{2,0,1:T(8,128)S(1)}, f32[16,32,4096]{2,0,1:T(8,128)}) fusion(f32[16,32,4096]{2,0,1:T(8,128)} %fusion.94, f32[16,32]{0,1:T(8,128)S(1)} %copy-done.11, f32[16,32]{0,1:T(8,128)S(1)} %get-tuple-element.38, f32[16,32,4096]{2,0,1:T(8,128)} %fusion.52, f32[16,32,4096]{2,1,0:T(8,128)} %reshape.362), kind=kOutput, calls=%fused_computation.52 | convolution fusion | flops 417336832 | bytes 41947136 | tf_op jit(solution)/shard_map/abm,ak->kbm/dot_general | solution.py:29
  700.8 18.0 %fusion.46 = f32[32,16,4096]{2,0,1:T(8,128)} fusion(f32[16,32,4096]{2,0,1:T(8,128)} %get-tuple-element.12), kind=kOutput, calls=%fused_computation.68 | convolution fusion | flops 805320704 | bytes 16777216 | tf_op jit(solution)/shard_map/kbm,bj->jkm/dot_general | solution.py:31
  731.4 16.0 subtract_multiply_fusion
  817.3 180.3 %all-to-all-done.1 = f32[2,512,32,128]{3,2,0,1:T(8,128)} async-done(((f32[2,512,32,128]{3,2,0,1:T(8,128)}), f32[2,512,32,128]{3,2,0,1:T(8,128)}, u32[]{:S(2)}, u32[]{:S(2)}) %all-to-all-start.1) | async-done | bytes 16777248 | tf_op jit(solution)/shard_map/all_to_all | solution.py:157
  1004.9 33.8 %fusion.19 = bf16[64,512,128]{2,1,0:T(8,128)(2,1)} fusion(bf16[64,512,128]{2,1,0:T(8,128)(2,1)} %param.11, f32[2,64,256,128]{3,2,0,1:T(8,128)S(1)} %bitcast.200, f32[128]{0:T(128)S(1)} %copy-done.18, f32[64,512]{1,0:T(8,128)S(1)} %copy-done.10, f32[64,512]{1,0:T(8,128)S(1)} %copy-done.8, f32[2,256,512,1]{1,2,0,3:T(8,128)S(1)} %maximum_bitcast_fusion.6), kind=kOutput, calls=%fused_computation.30 | convolution fusion | flops 25799163904 | bytes 34865664 | tf_op jit(solution)/shard_map/prkc,pkw->rwc/dot_general | solution.py:164
  1058.1 254.7 %all-gather.1 = bf16[4,1,512]{2,1,0:T(2,128)(2,1)S(1)} all-gather(bf16[1,1,512]{2,1,0:T(2,128)(2,1)S(1)} %reshape.373), channel_id=2, replica_groups=mesh['chan'=4,'rows'=8] {'chan'}, dimensions={0}, use_global_device_ids=true | all-gather | bytes 5120 | tf_op jit(solution)/shard_map/all_gather | solution.py:169
  1334.9 168.1 %fusion.325 = bf16[8192,2048]{1,0:T(8,128)(2,1)} fusion(f32[2048]{0:T(1024)S(1)} %bitcast.202, bf16[512,2048]{1,0:T(8,128)(2,1)} %all-gather.5.cloned.1.call-done, f32[64,8,64,128]{3,2,1,0:T(8,128)} %bitcast.187, f32[512]{0:T(512)S(1)} %copy-done.16, f32[8192]{0:T(1024)S(1)} %fusion.128, f32[8192]{0:T(1024)S(1)} %multiply_bitcast_fusion.4), kind=kOutput, calls=%fused_computation.3.clone.clone.clone.clone.1 | convolution fusion | flops 18303942656 | bytes 52504576 | tf_op jit(solution)/shard_map/dot_general | solution.py:110
  1503.0 24.4 %fusion.26 = bf16[8192,512]{1,0:T(8,128)(2,1)} fusion(bf16[2048,512]{1,0:T(8,128)(2,1)} %all-gather.7.cloned.1.call-done, bf16[8192,2048]{1,0:T(8,128)(2,1)} %fusion.325), kind=kOutput, calls=%fused_computation.44 | convolution fusion | flops 17184063488 | bytes 44040192 | tf_op jit(solution)/shard_map/dot_general | solution.py:114
  1545.3 180.7 %all-to-all-done.3 = bf16[64,128,512]{1,0,2:T(8,128)(2,1)} async-done(((bf16[64,128,512]{1,0,2:T(8,128)(2,1)}), bf16[64,128,512]{1,0,2:T(8,128)(2,1)}, u32[]{:S(2)}, u32[]{:S(2)}) %all-to-all-start.3) | async-done | bytes 8388640 | tf_op jit(solution)/shard_map/all_to_all | solution.py:175
  1749.3 17.4 copy.86
  (136 shorter events, 413.3 us)
Async XLA Ops:
  6.5 47.9 %copy-start.17 = (f32[128]{0:T(128)S(1)}, f32[128]{0:T(128)}, u32[]{:S(2)}) copy-start(f32[128]{0:T(128)} %param.12) | copy-start | bytes 1540
  6.5 46.2 %all-reduce.3.cloned.1.call-start = ((), (), s32[]{:S(2)}) async-start(), calls=%async_computation.6 | async-start | bytes 524288 | tf_op jit(solution)/shard_map/psum | solution.py:134
  109.1 7.3 copy-start.13
  109.1 188.9 %all-to-all-start = ((f32[2,64,256,128]{3,1,0,2:T(8,128)}), f32[2,64,256,128]{3,1,0,2:T(8,128)}, u32[]{:S(2)}, u32[]{:S(2)}) async-start(f32[2,64,256,128]{3,1,0,2:T(8,128)} %copy.51), calls=%async_computation | async-start | bytes 33554432 | tf_op jit(solution)/shard_map/all_to_all | solution.py:150
  329.9 17.1 copy-start.1
  409.2 18.1 %copy-start.4 = (f32[16,32,4096]{2,0,1:T(8,128)S(1)}, f32[16,32,4096]{2,0,1:T(8,128)}, u32[]{:S(2)}) copy-start(f32[16,32,4096]{2,0,1:T(8,128)} %get-tuple-element.14) | copy-start | bytes 25165828
  500.2 29.5 %slice-start.2 = ((s8[8388608]{0:T(1024)(128)(4,1)}), s8[4194304]{0:T(1024)(128)(4,1)S(1)}, s32[]{:S(2)}) async-start(s8[8388608]{0:T(1024)(128)(4,1)} %bitcast.183), calls=%async_computation.9 | async-start | bytes 8388608
  516.0 13.7 slice-start.3
  569.2 8.0 copy-start
  604.3 16.9 copy-start.2
  604.3 29.7 %slice-start = ((s8[8388608]{0:T(1024)(128)(4,1)}), s8[4194304]{0:T(1024)(128)(4,1)S(1)}, s32[]{:S(2)}) async-start(s8[8388608]{0:T(1024)(128)(4,1)} %bitcast.179), calls=%async_computation.7 | async-start | bytes 8388608
  604.3 29.7 %slice-start.4 = ((s8[8388608]{0:T(1024)(128)(4,1)}), s8[4194304]{0:T(1024)(128)(4,1)S(1)}, s32[]{:S(2)}) async-start(s8[8388608]{0:T(1024)(128)(4,1)} %bitcast.189), calls=%async_computation.11 | async-start | bytes 8388608
  621.2 12.8 slice-start.1
  621.2 12.8 slice-start.5
  621.2 12.8 copy-start.15
  660.8 18.1 %copy-start.11 = (f32[16,32]{0,1:T(8,128)S(1)}, f32[16,32]{0,1:T(8,128)}, u32[]{:S(2)}) copy-start(f32[16,32]{0,1:T(8,128)} %fusion.164) | copy-start | bytes 6148
  700.8 18.0 %copy-start.3 = (f32[16,32,4096]{2,0,1:T(8,128)S(1)}, f32[16,32,4096]{2,0,1:T(8,128)}, u32[]{:S(2)}) copy-start(f32[16,32,4096]{2,0,1:T(8,128)} %get-tuple-element.12) | copy-start | bytes 25165828
  781.8 13.7 slice-start.6
  807.5 190.1 %all-to-all-start.1 = ((f32[2,512,32,128]{3,2,0,1:T(8,128)}), f32[2,512,32,128]{3,2,0,1:T(8,128)}, u32[]{:S(2)}, u32[]{:S(2)}) async-start(f32[2,512,32,128]{3,2,0,1:T(8,128)} %copy.79), calls=%async_computation.1 | async-start | bytes 33554432 | tf_op jit(solution)/shard_map/all_to_all | solution.py:157
  1050.8 262.0 %all-to-all-start.2 = ((bf16[64,512,128]{2,0,1:T(8,128)(2,1)}), bf16[64,512,128]{2,0,1:T(8,128)(2,1)}, u32[]{:S(2)}, u32[]{:S(2)}) async-start(bf16[64,512,128]{2,0,1:T(8,128)(2,1)} %copy.82), calls=%async_computation.2 | async-start | bytes 16777216 | tf_op jit(solution)/shard_map/all_to_all | solution.py:166
  1056.6 278.3 %all-gather.5.cloned.1.call-start = ((), (), s32[]{:S(2)}) async-start(), calls=%async_computation.4 | async-start | bytes 2621440 | tf_op jit(solution)/shard_map/all_gather | solution.py:168
  1057.3 445.7 %all-gather.7.cloned.1.call-start = ((), (), s32[]{:S(2)}) async-start(), calls=%async_computation.5 | async-start | bytes 2621440 | tf_op jit(solution)/shard_map/all_gather | solution.py:171
  1327.4 7.5 copy-start.16
  1539.5 186.5 %all-to-all-start.3 = ((bf16[64,128,512]{1,0,2:T(8,128)(2,1)}), bf16[64,128,512]{1,0,2:T(8,128)(2,1)}, u32[]{:S(2)}, u32[]{:S(2)}) async-start(bf16[64,128,512]{1,0,2:T(8,128)(2,1)} %copy.84), calls=%async_computation.3 | async-start | bytes 16777216 | tf_op jit(solution)/shard_map/all_to_all | solution.py:175
  (11 other events, 61.1 us)
Sparse Core Ops, SparseCore 0:
  16.0 36.7 all-reduce.2
  1059.1 98.2 all-gather.4
  1159.0 102.3 all-gather.6
where the time goes:
time: 1800 us; the launch traced here: 1790 us
  matrix products  617 us (34%)
  waiting for transfers between devices  577 us (32%)
  blocking collectives  255 us (14%)
  local copies, waits for them, and re-layouts  246 us (14%)
  other arithmetic  51.3 us (3%)
  starting transfers between devices  25.5 us (1%)
    all_gather x1, blocking collectives, local(): lax.all_gather(fc1_bias[None, :], 'chan', axis=1, tiled=True)  255 us
    all_to_all x1, waiting for transfers between devices, local(): lax.all_to_all(local_out.reshape(row_count, grid_width // chan_count, all...  181 us
    all_to_all x1, waiting for transfers between devices, local(): lax.all_to_all(jnp.stack([back_real, back_imag]), 'rows', split_axis=1, c...  180 us
    all_to_all x1, waiting for transfers between devices, local(): lax.all_to_all(spectra, 'rows', split_axis=2, concat_axis=1, tiled=True)  180 us
    dot_general x1, matrix products, channel_mlp(): jnp.dot(normed, first_weight, preferred_element_type=jnp.float32)  168 us
    dot_general x4, matrix products, complex_sum(): first_sin = jnp.einsum(form, real_part, table_sin, precision=highest)  72.3 us
    dot_general x4, matrix products, complex_sum(): second_sin = jnp.einsum(form, imag_part, table_sin, precision=highest)  70.1 us
    dot_general x4, matrix products, complex_sum(): first_cos = jnp.einsum(form, real_part, table_cos, precision=highest)  68.1 us
  transfers between devices with their start and end apart: 7, of which 4 were waited for; matrix products, arithmetic and copies ran while one was open for 11% of the time, Pallas kernels for 0%

commit v1 on v0

v1 whole, which is shorter than its diff:
```python
import functools
import math

import jax
import jax.numpy as jnp
import numpy as np
from jax import lax
from jax.experimental import pallas as pl
from jax.experimental.pallas import tpu as pltpu
from jax.sharding import PartitionSpec as P

norm_eps = 1e-05
shrink_level = 0.01
spectral_chunks = 2
mlp_chunks = 4
bf16 = jnp.bfloat16
f32 = jnp.float32


def soften(values):
    return values - jnp.clip(values, -shrink_level, shrink_level)


def dft_tables(length):
    index = np.arange(length, dtype=np.int64)
    angle = 2.0 * np.pi / length * (index[:, None] * index[None, :] % length)
    scale = 1.0 / math.sqrt(length)
    return np.cos(angle) * scale, np.sin(angle) * scale


def dot(left, right):
    return jnp.dot(left, right, preferred_element_type=f32)


def spectral_kernel(x_ref, cos_ref, sin_ref, w1_ref, b1_ref, w2_ref, b2_ref, *rest):
    out_ref = rest[-1]
    parts, _, rows, lanes = x_ref.shape
    half = lanes // 2
    x = x_ref[...].reshape(parts * rows, lanes)
    turned = jnp.concatenate([x[:, half:], -x[:, :half]], axis=1)
    spectrum = dot(cos_ref[...], x) + dot(sin_ref[...], turned)
    first = jnp.maximum(dot(spectrum.astype(bf16), w1_ref[...]) + b1_ref[...], 0.0)
    second = dot(first.astype(bf16), w2_ref[...]) + b2_ref[...]
    shrunk = soften(second).astype(bf16)
    turned = jnp.concatenate([-shrunk[:, half:], shrunk[:, :half]], axis=1)
    back = dot(cos_ref[...], shrunk) + dot(sin_ref[...], turned)
    pieces, _, _, piece_rows, _ = out_ref.shape
    back = back.astype(bf16).reshape(parts, pieces, piece_rows, lanes)
    for i in range(pieces):
        out_ref[i, :, 0] = back[:, i]


def spectral_stage(x, cos_table, sin_table, w1, b1, w2, b2, pieces, own, first, held):
    parts, freqs, rows, lanes = x.shape
    length = parts * rows

    def whole(shape):
        return pl.BlockSpec(shape, lambda k: (0,) * len(shape))

    extra = [] if held is None else [held]
    return pl.pallas_call(
        spectral_kernel,
        grid=(freqs,),
        in_specs=[
            pl.BlockSpec((parts, 1, rows, lanes), lambda k: (0, k, 0, 0)),
            whole((length, length)),
            whole((length, length)),
            whole((lanes, lanes)),
            whole((1, lanes)),
            whole((lanes, lanes)),
            whole((1, lanes)),
        ]
        + [pl.BlockSpec(memory_space=pl.ANY)] * len(extra),
        out_specs=pl.BlockSpec(
            (pieces, parts, 1, rows // pieces, lanes), lambda k: (0, 0, first + k, 0, 0)
        ),
        out_shape=jax.ShapeDtypeStruct((pieces, parts, own, rows // pieces, lanes), bf16),
        input_output_aliases={7: 0} if extra else {},
        compiler_params=pltpu.CompilerParams(vmem_limit_bytes=32 * 2**20),
        cost_estimate=pl.CostEstimate(
            flops=freqs * (8 * length * length * lanes + 4 * length * lanes * lanes),
            bytes_accessed=4 * x.size,
            transcendentals=0,
        ),
    )(x, cos_table, sin_table, w1, b1, w2, b2, *extra)


def mlp_kernel(count, *refs):
    x_refs, (gain_ref, w1_ref, b1_ref, w2_ref), out_refs = (
        refs[:count],
        refs[count : count + 4],
        refs[count + 4 :],
    )
    x = jnp.concatenate([ref[...] for ref in x_refs], axis=1).astype(f32)
    center = jnp.mean(x, axis=-1, keepdims=True)
    spread = jnp.mean(x * x, axis=-1, keepdims=True) - center * center
    normed = ((x - center) * lax.rsqrt(spread + norm_eps) * gain_ref[...]).astype(bf16)
    total = None
    for i in range(w1_ref.shape[0]):
        hidden = dot(normed, w1_ref[i]) + b1_ref[i].astype(f32)
        hidden = (0.5 * hidden * (1.0 + lax.erf(hidden * (1.0 / math.sqrt(2.0))))).astype(bf16)
        term = dot(hidden, w2_ref[i])
        total = term if total is None else total + term
    for i, ref in enumerate(out_refs):
        chan = ref.shape[1]
        ref[...] = total[:, i * chan : (i + 1) * chan].astype(bf16)


def mlp_stage(pieces, gain, w1, b1, w2):
    tokens, chan = pieces[0].shape
    count = len(pieces)
    step = min(512, tokens)
    block = pl.BlockSpec((step, chan), lambda t: (t, 0))

    def whole(array):
        return pl.BlockSpec(array.shape, lambda t: (0,) * array.ndim)

    return pl.pallas_call(
        functools.partial(mlp_kernel, count),
        grid=(tokens // step,),
        in_specs=[block] * count + [whole(gain), whole(w1), whole(b1), whole(w2)],
        out_specs=[block] * count,
        out_shape=[jax.ShapeDtypeStruct((tokens, chan), bf16)] * count,
        compiler_params=pltpu.CompilerParams(vmem_limit_bytes=40 * 2**20),
        cost_estimate=pl.CostEstimate(
            flops=4 * tokens * w1.size,
            bytes_accessed=4 * count * tokens * chan,
            transcendentals=0,
        ),
    )(*pieces, gain, w1, b1, w2)


def layer_matrix(weights):
    count, size = weights.shape[1], weights.shape[2]
    eye = jnp.eye(count, dtype=weights.dtype)
    real, imag = (
        (part[:, :, None, :] * eye[:, None, :, None]).reshape(count * size, count * size)
        for part in (weights[0], weights[1])
    )
    return jnp.concatenate(
        [jnp.concatenate([real, imag], 1), jnp.concatenate([-imag, real], 1)], 0
    ).astype(bf16)


def local(
    tokens,
    gain_in,
    spectral_w1,
    spectral_b1,
    spectral_w2,
    spectral_b2,
    gain_out,
    fc1_weight,
    fc1_bias,
    fc2_weight,
    fc2_bias,
):
    row_count, width, chan = tokens.shape
    row_parts = lax.axis_size("rows")
    chan_parts = lax.axis_size("chan")
    all_channels = chan * chan_parts
    height = row_count * row_parts
    half = width // 2
    own = half // row_parts

    source = tokens.astype(f32)
    totals, squares = lax.psum((jnp.sum(source, axis=2), jnp.sum(source * source, axis=2)), "chan")
    fc1_weight, fc2_weight, fc1_bias, totals = lax.optimization_barrier(
        (fc1_weight, fc2_weight, fc1_bias, totals)
    )
    fc1_full = lax.all_gather(fc1_weight, "chan")
    fc2_full = lax.all_gather(fc2_weight, "chan")
    bias_full = lax.all_gather(fc1_bias[None, :], "chan")
    center = (totals / all_channels)[:, :, None]
    spread = (squares / all_channels)[:, :, None] - center * center
    normed = (source - center) * lax.rsqrt(spread + norm_eps) * gain_in
    normed_low = normed.astype(bf16)

    cos_w, sin_w = dft_tables(width)
    cos_h, sin_h = dft_tables(height)
    forward = np.stack([cos_w[:half], -sin_w[:half]], 1)
    weighting = np.where(np.arange(half) == 0, 1.0, 2.0)[:, None, None]
    inverse = forward * weighting
    shape = (row_parts, spectral_chunks, own // spectral_chunks, 2, width)
    forward = jnp.asarray(forward.reshape(shape), bf16)
    inverse = jnp.asarray(inverse.reshape(shape), bf16)
    cos_h = jnp.asarray(cos_h, bf16)
    sin_h = jnp.asarray(sin_h, bf16)
    w1, w2 = layer_matrix(spectral_w1), layer_matrix(spectral_w2)
    b1, b2 = spectral_b1.reshape(1, -1), spectral_b2.reshape(1, -1)

    pieces = max(1, min(mlp_chunks, row_count // 16))
    rows = row_count // pieces
    group = own // spectral_chunks
    back = None
    for j in range(spectral_chunks):
        spectra = jnp.einsum(
            "rwc,dkpw->dkrpc", normed_low, forward[:, j], preferred_element_type=f32
        ).astype(bf16)
        spectra = spectra.reshape(row_parts, group, row_count, 2 * chan)
        columns = lax.all_to_all(spectra, "rows", split_axis=0, concat_axis=0, tiled=True)
        if j == spectral_chunks - 1:
            columns, fc1_full, fc2_full, bias_full = lax.optimization_barrier(
                (columns, fc1_full, fc2_full, bias_full)
            )
        back = spectral_stage(
            columns, cos_h, sin_h, w1, b1, w2, b2, pieces, own, j * group, back
        )

    me = lax.axis_index("chan")

    def turned(values, axis):
        starts = [lax.rem(me + chan_parts - s, chan_parts) * chan for s in range(chan_parts)]
        blocks = [lax.dynamic_slice_in_dim(values, start, chan, axis) for start in starts]
        return jnp.concatenate(blocks, axis)

    gain_turned = turned(gain_out, 0).reshape(1, all_channels)
    fc1_turned = turned(fc1_full, 1)
    fc2_turned = turned(fc2_full, 2)
    part = width // chan_parts
    places = [lax.rem(me + s, chan_parts) * part for s in range(chan_parts)]

    def turn(values, shift):
        if shift % chan_parts == 0:
            return values
        pairs = [(i, (i + shift) % chan_parts) for i in range(chan_parts)]
        return lax.ppermute(values, "chan", pairs)

    out = jnp.zeros(tokens.shape, bf16)
    table = inverse.reshape(row_parts, own, 2, width)
    for j in range(pieces):
        returned = lax.all_to_all(back[j], "rows", split_axis=0, concat_axis=0, tiled=True)
        returned = returned.reshape(row_parts, own, rows, 2, chan)
        filtered = jnp.einsum("dkrpc,dkpw->rwc", returned, table, preferred_element_type=f32)
        span = slice(j * rows, (j + 1) * rows)
        mixed = (filtered + normed[span] + source[span]).astype(bf16)
        kept = [lax.dynamic_slice_in_dim(mixed, place, part, 1) for place in places]
        full = [turn(kept[s].reshape(rows * part, chan), s) for s in range(chan_parts)]
        done = mlp_stage(full, gain_turned, fc1_turned, bias_full, fc2_turned)
        for s in range(chan_parts):
            summed = turn(done[s], -s).reshape(rows, part, chan)
            final = (kept[s].astype(f32) + summed.astype(f32) + fc2_bias.astype(f32)).astype(bf16)
            out = lax.dynamic_update_slice(out, final, (j * rows, places[s], 0))
    return out


def solution(mesh):
    return jax.shard_map(
        local,
        mesh=mesh,
        in_specs=(
            P("rows", None, "chan"),
            P("chan"),
            P(None, "chan", None, None),
            P(None, "chan", None),
            P(None, "chan", None, None),
            P(None, "chan", None),
            P(),
            P(None, "chan"),
            P("chan"),
            P("chan", None),
            P("chan"),
        ),
        out_specs=P("rows", None, "chan"),
        check_vma=False,
    )
```

time: 1800 us -> 776 us (0.43)
  matrix products: 617 us -> 36.9 us
  waiting for transfers between devices: 577 us -> 154 us
  blocking collectives: 255 us -> 41.1 us
  starting transfers between devices: 25.5 us -> 191 us
  Pallas kernels: 0 us -> 102 us
  local copies, waits for them, and re-layouts: 246 us -> 173 us
    dot_general x28 -> x6, matrix products: 617 us -> 36.9 us  [the longest x4 23.2 us: local(): jnp.einsum('dkrpc,dkpw->rwc', returned, table, preferred_element_type=f32)]
    all_to_all x4 -> x5, waiting for transfers between devices: 541 us -> 43.8 us  [the longest x2 26 us: local(): lax.all_to_all(spectra, 'rows', split_axis=0, concat_axis=0, tiled=True)]
    all_gather x1, blocking collectives: 255 us -> 11.9 us  [local(): bias_full = lax.all_gather(fc1_bias[None, :], 'chan')]
    ppermute x0 -> x24, starting transfers between devices: none -> 163 us  [turn(): return lax.ppermute(values, 'chan', pairs)]
    pallas_call x0 -> x6, Pallas kernels: none -> 102 us  [the longest x2 52.1 us: spectral_stage(): pl.pallas_call(spectral_kernel, grid=(freqs,), in_specs=[pl.BlockSpec((pa...]
    mul x4 -> x1, local copies, waits for them, and re-layouts: 39.7 us -> 0.02 us  [layer_matrix(): part[:, :, None, :] * eye[:, None, :, None]]
    dynamic_slice x0 -> x23, local copies, waits for them, and re-layouts: none -> 38.1 us  [the longest x20 36 us: local(): kept = [lax.dynamic_slice_in_dim(mixed, place, part, 1) for place in places]]
    ppermute x0 -> x24, waiting for transfers between devices: none -> 37.2 us  [turn(): return lax.ppermute(values, 'chan', pairs)]
  transfers between devices with their start and end apart: 7 -> 32, of which waited for: 4 -> 10; matrix products, arithmetic and copies ran while one was open for 11% -> 22% of each run, Pallas kernels for 0% -> 7%
where the time goes in v1:
time: 776 us; the launch traced here: 763 us
  starting transfers between devices  191 us (25%)
  local copies, waits for them, and re-layouts  173 us (22%)
  waiting for transfers between devices  154 us (20%)
  Pallas kernels  102 us (13%)
  other arithmetic  50.5 us (7%)
  blocking collectives  41.1 us (5%)
  matrix products  36.9 us (5%)
  between operations  14.3 us (2%)
    ppermute x24, starting transfers between devices, turn(): return lax.ppermute(values, 'chan', pairs)  163 us
    pallas_call x2, Pallas kernels, spectral_stage(): pl.pallas_call(spectral_kernel, grid=(freqs,), in_specs=[pl.BlockSpec((pa...  52.1 us
    pallas_call x4, Pallas kernels, mlp_stage(): pl.pallas_call(functools.partial(mlp_kernel, count), grid=(tokens // step...  50.3 us
    ppermute x24, waiting for transfers between devices, turn(): return lax.ppermute(values, 'chan', pairs)  37.2 us
    psum x1, waiting for transfers between devices, local(): lax.psum((jnp.sum(source, axis=2), jnp.sum(source * source, axis=2)), 'ch...  36.9 us
    dynamic_slice x20, local copies, waits for them, and re-layouts, local(): kept = [lax.dynamic_slice_in_dim(mixed, place, part, 1) for place in places]  36 us
    all_gather x1, waiting for transfers between devices, local(): fc2_full = lax.all_gather(fc2_weight, 'chan')  34.4 us
    convert_element_type x16, local copies, waits for them, and re-layouts, local(): summed.astype(f32)  31 us
  transfers between devices with their start and end apart: 32, of which 10 were waited for; matrix products, arithmetic and copies ran while one was open for 22% of the time, Pallas kernels for 7%

profile of v1, /device:TPU:2, one launch (start us, length us, event | category | flops | bytes accessed | tf_op | source)
XLA Modules:
  0.0 762.8 jit_solution(8887304922807459081)
XLA Ops:
  6.5 11.9 %copy.74 = bf16[64,512,128]{1,2,0:T(8,128)(2,1)} copy(bf16[64,512,128]{2,1,0:T(8,128)(2,1)} %param.15) | data formatting | bytes 16777216 | tf_op args[0]
  18.4 9.0 %convert_reduce_fusion = (f32[64,512]{1,0:T(8,128)}, f32[64,512]{1,0:T(8,128)}) fusion(bf16[64,512,128]{1,2,0:T(8,128)(2,1)} %copy.74), kind=kLoop, calls=%fused_computation.2 | loop fusion | flops 16711680 | bytes 8650752 | tf_op jit(solution)/shard_map/reduce_sum | solution.py:167
  27.5 36.9 %all-reduce.3.cloned.1.call-done = (f32[64,512]{1,0:T(8,128)}, f32[64,512]{1,0:T(8,128)}) async-done(((f32[64,512]{1,0:T(8,128)}, f32[64,512]{1,0:T(8,128)}), (f32[64,512]{1,0:T(8,128)}, f32[64,512]{1,0:T(8,128)})) %all-reduce.3.cloned.1.call-update) | async-done | bytes 262160 | tf_op jit(solution)/shard_map/psum | solution.py:167
  113.4 26.0 %all-to-all-done.x_ref = bf16[8,16,64,256]{3,2,1,0:T(8,128)(2,1)} async-done(((bf16[8,16,64,256]{3,2,1,0:T(8,128)(2,1)}), bf16[8,16,64,256]{3,2,1,0:T(8,128)(2,1)}, u32[]{:S(2)}, u32[]{:S(2)}) %all-to-all-start) | async-done | bytes 4194336 | tf_op jit(solution)/shard_map/all_to_all | solution.py:201
  147.3 11.9 %all-gather.3.refs_6_ = bf16[4,1,512]{2,1,0:T(2,128)(2,1)S(1)} all-gather(bf16[1,1,512]{2,1,0:T(2,128)(2,1)S(1)} %reshape.215), channel_id=4, replica_groups=mesh['chan'=4,'rows'=8] {'chan'}, dimensions={0}, use_global_device_ids=true | all-gather | bytes 5120 | tf_op jit(solution)/shard_map/all_gather | solution.py:173
  159.2 34.4 %all-gather.9.cloned.1.call-done = bf16[2048,512]{1,0:T(8,128)(2,1)} async-done(((bf16[512,512]{1,0:T(8,128)(2,1)}), bf16[2048,512]{1,0:T(8,128)(2,1)}) %all-gather.9.cloned.1.call-update) | async-done | bytes 2097168 | tf_op jit(solution)/shard_map/all_gather | solution.py:172
  193.6 26.0 %shard_map.145.rest_0_ = bf16[4,8,32,16,256]{4,3,2,1,0:T(8,128)(2,1)S(1)} custom-call(bf16[8,16,64,256]{3,2,1,0:T(8,128)(2,1)} %all-to-all-done.1.x_ref, bf16[512,512]{1,0:T(8,128)(2,1)S(1)} %copy-done.23, bf16[512,512]{1,0:T(8,128)(2,1)S(1)} %copy-done.24, bf16[256,256]{1,0:T(8,128)(2,1)S(1)} %maximum_maximum_fusion.w1_ref, f32[1,256]{1,0:T(1,128)S(1)} %reshape.163.b1_ref, ...), custom_call_target="tpu_custom_call" | custom-call | flops 10737418240 | bytes 8388608 | tf_op jit(solution)/shard_map/pallas_call | solution.py:61
  219.6 26.1 %shard_map.146 = bf16[4,8,32,16,256]{4,3,2,1,0:T(8,128)(2,1)S(1)} custom-call(bf16[8,16,64,256]{3,2,1,0:T(8,128)(2,1)} %all-to-all-done.x_ref, bf16[512,512]{1,0:T(8,128)(2,1)S(1)} %copy-done.23, bf16[512,512]{1,0:T(8,128)(2,1)S(1)} %copy-done.24, bf16[256,256]{1,0:T(8,128)(2,1)S(1)} %maximum_maximum_fusion.w1_ref, ...), custom_call_target="tpu_custom_call", output_to_operand_aliasing={{}: (7, {})} | custom-call | flops 10737418240 | bytes 8388608 | tf_op jit(solution)/shard_map/pallas_call | solution.py:61
  248.5 29.3 %all_to_all.30 = bf16[8,32,16,256]{3,2,1,0:T(8,128)(2,1)} all-to-all(bf16[8,32,16,256]{3,2,1,0:T(8,128)(2,1)S(1)} %get-tuple-element.59), channel_id=1, replica_groups=mesh['chan'=4,'rows'=8] {'rows'}, dimensions={0} | all-to-all | bytes 4194304 | tf_op jit(solution)/shard_map/all_to_all | solution.py:232
  283.2 11.6 %convert_element_type.256 = f32[64,512,128]{1,2,0:T(8,128)} convert(bf16[64,512,128]{1,2,0:T(8,128)(2,1)} %copy.74) | non-fusion elementwise | flops 4194304 | bytes 25165824 | tf_op jit(solution)/shard_map/convert_element_type | solution.py:166
  294.9 13.3 %all-to-all-done.2 = bf16[8,32,16,256]{3,2,1,0:T(8,128)(2,1)S(1)} async-done(((bf16[8,32,16,256]{3,2,1,0:T(8,128)(2,1)}), bf16[8,32,16,256]{3,2,1,0:T(8,128)(2,1)S(1)}, u32[]{:S(2)}, u32[]{:S(2)}) %all-to-all-start.2) | async-done | bytes 2097184 | tf_op jit(solution)/shard_map/all_to_all | solution.py:232
  314.0 12.7 %multiply_multiply_fusion = f32[64,512,128]{1,2,0:T(8,128)} fusion(bf16[64,512,128]{1,2,0:T(8,128)(2,1)} %copy.74, f32[128]{0:T(128)S(1)} %copy-done.67, f32[64,512]{1,0:T(8,128)S(1)} %get-tuple-element.90, f32[64,512]{1,0:T(8,128)S(1)} %get-tuple-element.89), kind=kLoop, calls=%fused_computation | loop fusion | flops 16777216 | bytes 25428480 | tf_op jit(solution)/shard_map/mul | solution.py:176
  431.8 12.9 %shard_map.148 = (bf16[2048,128]{1,0:T(8,128)(2,1)S(1)}, bf16[2048,128]{1,0:T(8,128)(2,1)}, bf16[2048,128]{1,0:T(8,128)(2,1)S(1)}, bf16[2048,128]{1,0:T(8,128)(2,1)S(1)}) custom-call(bf16[2048,128]{1,0:T(8,128)(2,1)S(1)} %bitcast.131, bf16[2048,128]{1,0:T(8,128)(2,1)S(1)} %copy-done.18, bf16[2048,128]{1,0:T(8,128)(2,1)} %collective-permute-done.7.refs_2_, ...), custom_call_target="tpu_custom_call" | custom-call | flops 8589934592 | bytes 4194304 | tf_op jit(solution)/shard_map/pallas_call | solution.py:118
  450.8 9.2 %collective-permute-done.2.refs_3_ = bf16[2048,128]{1,0:T(8,128)(2,1)} collective-permute-done((bf16[2048,128]{1,0:T(8,128)(2,1)}, bf16[2048,128]{1,0:T(8,128)(2,1)}, u32[]{:S(2)}, u32[]{:S(2)}) %collective-permute-start.2) | collective-permute-done | bytes 524320 | tf_op jit(solution)/shard_map/ppermute | solution.py:227
  461.7 13.2 %shard_map.147 = (bf16[2048,128]{1,0:T(8,128)(2,1)S(1)}, bf16[2048,128]{1,0:T(8,128)(2,1)}, bf16[2048,128]{1,0:T(8,128)(2,1)}, bf16[2048,128]{1,0:T(8,128)(2,1)}) custom-call(bf16[2048,128]{1,0:T(8,128)(2,1)S(1)} %bitcast.129, bf16[2048,128]{1,0:T(8,128)(2,1)} %collective-permute-done.refs_1_, bf16[2048,128]{1,0:T(8,128)(2,1)} %collective-permute-done.1.refs_2_, ...), custom_call_target="tpu_custom_call" | custom-call | flops 8589934592 | bytes 4194304 | tf_op jit(solution)/shard_map/pallas_call | solution.py:118
  474.9 34.0 %collective-permute-start.14 = (bf16[2048,128]{1,0:T(8,128)(2,1)S(1)}, bf16[2048,128]{1,0:T(8,128)(2,1)S(1)}, u32[]{:S(2)}, u32[]{:S(2)}) collective-permute-start(bf16[2048,128]{1,0:T(8,128)(2,1)S(1)} %bitcast.140), channel_id=1, source_target_pairs={{0,24},{8,0},{16,8},{24,16},{1,25},{9,1},{17,9},{25,17},{2,26},{10... | collective-permute-start | bytes 1572872 | tf_op jit(solution)/shard_map/ppermute | solution.py:227
  515.4 12.3 %collective-permute-start.10 = (bf16[2048,128]{1,0:T(8,128)(2,1)S(1)}, bf16[2048,128]{1,0:T(8,128)(2,1)S(1)}, u32[]{:S(2)}, u32[]{:S(2)}) collective-permute-start(bf16[2048,128]{1,0:T(8,128)(2,1)S(1)} %copy-done.22), channel_id=1, source_target_pairs={{0,16},{8,24},{16,0},{24,8},{1,17},{9,25},{17,1},{25,9},{2,18},{10... | collective-permute-start | bytes 1572872 | tf_op jit(solution)/shard_map/ppermute | solution.py:227
  527.7 23.1 %collective-permute-start.11 = (bf16[2048,128]{1,0:T(8,128)(2,1)S(1)}, bf16[2048,128]{1,0:T(8,128)(2,1)S(1)}, u32[]{:S(2)}, u32[]{:S(2)}) collective-permute-start(bf16[2048,128]{1,0:T(8,128)(2,1)S(1)} %copy-done.16), channel_id=1, source_target_pairs={{0,8},{8,16},{16,24},{24,0},{1,9},{9,17},{17,25},{25,1},{2,10},{10... | collective-permute-start | bytes 1572872 | tf_op jit(solution)/shard_map/ppermute | solution.py:227
  550.7 12.0 %shard_map.150 = (bf16[2048,128]{1,0:T(8,128)(2,1)S(1)}, bf16[2048,128]{1,0:T(8,128)(2,1)S(1)}, bf16[2048,128]{1,0:T(8,128)(2,1)S(1)}, bf16[2048,128]{1,0:T(8,128)(2,1)}) custom-call(bf16[2048,128]{1,0:T(8,128)(2,1)S(1)} %bitcast.130, bf16[2048,128]{1,0:T(8,128)(2,1)S(1)} %collective-permute-done.18.refs_1_, ...), custom_call_target="tpu_custom_call" | custom-call | flops 8589934592 | bytes 4194304 | tf_op jit(solution)/shard_map/pallas_call | solution.py:118
  574.3 33.8 %collective-permute-start.23 = (bf16[2048,128]{1,0:T(8,128)(2,1)}, bf16[2048,128]{1,0:T(8,128)(2,1)}, u32[]{:S(2)}, u32[]{:S(2)}) collective-permute-start(bf16[2048,128]{1,0:T(8,128)(2,1)} %get-tuple-element.52), channel_id=1, source_target_pairs={{0,8},{8,16},{16,24},{24,0},{1,9},{9,17},{17,25},{25,1},{2,10},{10... | collective-permute-start | bytes 1572872 | tf_op jit(solution)/shard_map/ppermute | solution.py:227
  608.1 12.2 %shard_map.149 = (bf16[2048,128]{1,0:T(8,128)(2,1)S(1)}, bf16[2048,128]{1,0:T(8,128)(2,1)S(1)}, bf16[2048,128]{1,0:T(8,128)(2,1)S(1)}, bf16[2048,128]{1,0:T(8,128)(2,1)S(1)}) custom-call(bf16[2048,128]{1,0:T(8,128)(2,1)S(1)} %bitcast.128, bf16[2048,128]{1,0:T(8,128)(2,1)} %collective-permute-done.12.refs_1_, ...), custom_call_target="tpu_custom_call" | custom-call | flops 8589934592 | bytes 4194304 | tf_op jit(solution)/shard_map/pallas_call | solution.py:118
  649.0 34.1 %collective-permute-start.22 = (bf16[2048,128]{1,0:T(8,128)(2,1)S(1)}, bf16[2048,128]{1,0:T(8,128)(2,1)}, u32[]{:S(2)}, u32[]{:S(2)}) collective-permute-start(bf16[2048,128]{1,0:T(8,128)(2,1)S(1)} %copy-done.8), channel_id=1, source_target_pairs={{0,16},{8,24},{16,0},{24,8},{1,17},{9,25},{17,1},{25,9},{2,18},{10... | collective-permute-start | bytes 1572872 | tf_op jit(solution)/shard_map/ppermute | solution.py:227
  685.4 8.3 %add_convert_fusion = (bf16[16,128,128]{1,2,0:T(8,128)(2,1)}, bf16[16,128,128]{1,2,0:T(8,128)(2,1)}, bf16[16,128,128]{1,2,0:T(8,128)(2,1)}, bf16[16,128,128]{1,2...) fusion(f32[16,128,128]{1,2,0:T(8,128)} %copy.129, ...), kind=kLoop, calls=%fused_computation.33 | loop fusion | flops 9437184 | bytes 18874880 | tf_op jit(solution)/shard_map/convert_element_type | solution.py:242
  704.9 14.1 %collective-permute-done.22 = bf16[2048,128]{1,0:T(8,128)(2,1)} collective-permute-done((bf16[2048,128]{1,0:T(8,128)(2,1)S(1)}, bf16[2048,128]{1,0:T(8,128)(2,1)}, u32[]{:S(2)}, u32[]{:S(2)}) %collective-permute-start.22) | collective-permute-done | bytes 524320 | tf_op jit(solution)/shard_map/ppermute | solution.py:227
  (304 shorter events, 280.1 us)
Async XLA Ops:
  6.5 57.9 %all-reduce.3.cloned.1.call-start = ((), (), s32[]{:S(2)}) async-start(), calls=%async_computation.8 | async-start | bytes 524288 | tf_op jit(solution)/shard_map/psum | solution.py:167
  91.7 67.5 %all-gather.7.cloned.1.call-start = ((), (), s32[]{:S(2)}) async-start(), calls=%async_computation.6 | async-start | bytes 2621440 | tf_op jit(solution)/shard_map/all_gather | solution.py:171
  139.4 54.2 %all-to-all-start.1 = ((bf16[8,16,64,256]{3,2,1,0:T(8,128)(2,1)}), bf16[8,16,64,256]{3,2,1,0:T(8,128)(2,1)}, u32[]{:S(2)}, u32[]{:S(2)}) async-start(bf16[8,16,64,256]{3,2,1,0:T(8,128)(2,1)} %reshape.165), calls=%async_computation.1 | async-start | bytes 8388608 | tf_op jit(solution)/shard_map/all_to_all | solution.py:201
  339.3 63.8 %all-to-all-start.5 = ((bf16[8,32,16,256]{3,2,1,0:T(8,128)(2,1)}), bf16[8,32,16,256]{3,2,1,0:T(8,128)(2,1)}, u32[]{:S(2)}, u32[]{:S(2)}) async-start(bf16[8,32,16,256]{3,2,1,0:T(8,128)(2,1)} %get-tuple-element.57), calls=%async_computation.5 | async-start | bytes 4194304 | tf_op jit(solution)/shard_map/all_to_all | solution.py:232
  353.1 69.5 %collective-permute-start.6 = (bf16[2048,128]{1,0:T(8,128)(2,1)}, bf16[2048,128]{1,0:T(8,128)(2,1)S(1)}, u32[]{:S(2)}, u32[]{:S(2)}) collective-permute-start(bf16[2048,128]{1,0:T(8,128)(2,1)} %bitcast.150), channel_id=1, source_target_pairs={{0,8},{8,16},{16,24},{24,0},{1,9},{9,17},{17,25},{25,1},{2,10},{10... | collective-permute-start | bytes 1572872 | tf_op jit(solution)/shard_map/ppermute | solution.py:227
  356.5 69.5 %collective-permute-start.7 = (bf16[2048,128]{1,0:T(8,128)(2,1)}, bf16[2048,128]{1,0:T(8,128)(2,1)}, u32[]{:S(2)}, u32[]{:S(2)}) collective-permute-start(bf16[2048,128]{1,0:T(8,128)(2,1)} %bitcast.148), channel_id=1, source_target_pairs={{0,16},{8,24},{16,0},{24,8},{1,17},{9,25},{17,1},{25,9},{2,18},{10... | collective-permute-start | bytes 1572872 | tf_op jit(solution)/shard_map/ppermute | solution.py:227
  360.0 66.6 %collective-permute-start.8 = (bf16[2048,128]{1,0:T(8,128)(2,1)}, bf16[2048,128]{1,0:T(8,128)(2,1)}, u32[]{:S(2)}, u32[]{:S(2)}) collective-permute-start(bf16[2048,128]{1,0:T(8,128)(2,1)} %bitcast.147), channel_id=1, source_target_pairs={{0,24},{8,0},{16,8},{24,16},{1,25},{9,1},{17,9},{25,17},{2,26},{10... | collective-permute-start | bytes 1572872 | tf_op jit(solution)/shard_map/ppermute | solution.py:227
  377.6 69.8 %collective-permute-start = (bf16[2048,128]{1,0:T(8,128)(2,1)}, bf16[2048,128]{1,0:T(8,128)(2,1)}, u32[]{:S(2)}, u32[]{:S(2)}) collective-permute-start(bf16[2048,128]{1,0:T(8,128)(2,1)} %bitcast.146), channel_id=1, source_target_pairs={{0,8},{8,16},{16,24},{24,0},{1,9},{9,17},{17,25},{25,1},{2,10},{10... | collective-permute-start | bytes 1572872 | tf_op jit(solution)/shard_map/ppermute | solution.py:227
  379.7 70.0 %collective-permute-start.1 = (bf16[2048,128]{1,0:T(8,128)(2,1)}, bf16[2048,128]{1,0:T(8,128)(2,1)}, u32[]{:S(2)}, u32[]{:S(2)}) collective-permute-start(bf16[2048,128]{1,0:T(8,128)(2,1)} %bitcast.144), channel_id=1, source_target_pairs={{0,16},{8,24},{16,0},{24,8},{1,17},{9,25},{17,1},{25,9},{2,18},{10... | collective-permute-start | bytes 1572872 | tf_op jit(solution)/shard_map/ppermute | solution.py:227
  426.0 137.6 %collective-permute-start.12 = (bf16[2048,128]{1,0:T(8,128)(2,1)}, bf16[2048,128]{1,0:T(8,128)(2,1)}, u32[]{:S(2)}, u32[]{:S(2)}) collective-permute-start(bf16[2048,128]{1,0:T(8,128)(2,1)} %bitcast.142), channel_id=1, source_target_pairs={{0,8},{8,16},{16,24},{24,0},{1,9},{9,17},{17,25},{25,1},{2,10},{10... | collective-permute-start | bytes 1572872 | tf_op jit(solution)/shard_map/ppermute | solution.py:227
  426.6 137.0 %collective-permute-start.13 = (bf16[2048,128]{1,0:T(8,128)(2,1)}, bf16[2048,128]{1,0:T(8,128)(2,1)}, u32[]{:S(2)}, u32[]{:S(2)}) collective-permute-start(bf16[2048,128]{1,0:T(8,128)(2,1)} %bitcast.141), channel_id=1, source_target_pairs={{0,16},{8,24},{16,0},{24,8},{1,17},{9,25},{17,1},{25,9},{2,18},{10... | collective-permute-start | bytes 1572872 | tf_op jit(solution)/shard_map/ppermute | solution.py:227
  449.7 65.7 %collective-permute-start.19 = (bf16[2048,128]{1,0:T(8,128)(2,1)}, bf16[2048,128]{1,0:T(8,128)(2,1)S(1)}, u32[]{:S(2)}, u32[]{:S(2)}) collective-permute-start(bf16[2048,128]{1,0:T(8,128)(2,1)} %bitcast.149), channel_id=1, source_target_pairs={{0,16},{8,24},{16,0},{24,8},{1,17},{9,25},{17,1},{25,9},{2,18},{10... | collective-permute-start | bytes 1572872 | tf_op jit(solution)/shard_map/ppermute | solution.py:227
  460.1 67.6 %collective-permute-start.20 = (bf16[2048,128]{1,0:T(8,128)(2,1)}, bf16[2048,128]{1,0:T(8,128)(2,1)S(1)}, u32[]{:S(2)}, u32[]{:S(2)}) collective-permute-start(bf16[2048,128]{1,0:T(8,128)(2,1)} %bitcast.145), channel_id=1, source_target_pairs={{0,24},{8,0},{16,8},{24,16},{1,25},{9,1},{17,9},{25,17},{2,26},{10... | collective-permute-start | bytes 1572872 | tf_op jit(solution)/shard_map/ppermute | solution.py:227
  474.9 90.2 %collective-permute-start.14 = (bf16[2048,128]{1,0:T(8,128)(2,1)S(1)}, bf16[2048,128]{1,0:T(8,128)(2,1)S(1)}, u32[]{:S(2)}, u32[]{:S(2)}) collective-permute-start(bf16[2048,128]{1,0:T(8,128)(2,1)S(1)} %bitcast.140), channel_id=1, source_target_pairs={{0,24},{8,0},{16,8},{24,16},{1,25},{9,1},{17,9},{25,17},{2,26},{10... | collective-permute-start | bytes 1572872 | tf_op jit(solution)/shard_map/ppermute | solution.py:227
  563.6 68.2 %collective-permute-start.9 = (bf16[2048,128]{1,0:T(8,128)(2,1)}, bf16[2048,128]{1,0:T(8,128)(2,1)}, u32[]{:S(2)}, u32[]{:S(2)}) collective-permute-start(bf16[2048,128]{1,0:T(8,128)(2,1)} %get-tuple-element.42), channel_id=1, source_target_pairs={{0,24},{8,0},{16,8},{24,16},{1,25},{9,1},{17,9},{25,17},{2,26},{10... | collective-permute-start | bytes 1572872 | tf_op jit(solution)/shard_map/ppermute | solution.py:227
  563.6 70.6 %collective-permute-start.3 = (bf16[2048,128]{1,0:T(8,128)(2,1)}, bf16[2048,128]{1,0:T(8,128)(2,1)}, u32[]{:S(2)}, u32[]{:S(2)}) collective-permute-start(bf16[2048,128]{1,0:T(8,128)(2,1)} %get-tuple-element.38), channel_id=1, source_target_pairs={{0,24},{8,0},{16,8},{24,16},{1,25},{9,1},{17,9},{25,17},{2,26},{10... | collective-permute-start | bytes 1572872 | tf_op jit(solution)/shard_map/ppermute | solution.py:227
  565.1 75.4 %collective-permute-start.4 = (bf16[2048,128]{1,0:T(8,128)(2,1)}, bf16[2048,128]{1,0:T(8,128)(2,1)}, u32[]{:S(2)}, u32[]{:S(2)}) collective-permute-start(bf16[2048,128]{1,0:T(8,128)(2,1)} %get-tuple-element.39), channel_id=1, source_target_pairs={{0,16},{8,24},{16,0},{24,8},{1,17},{9,25},{17,1},{25,9},{2,18},{10... | collective-permute-start | bytes 1572872 | tf_op jit(solution)/shard_map/ppermute | solution.py:227
  567.1 76.2 %collective-permute-start.5 = (bf16[2048,128]{1,0:T(8,128)(2,1)}, bf16[2048,128]{1,0:T(8,128)(2,1)}, u32[]{:S(2)}, u32[]{:S(2)}) collective-permute-start(bf16[2048,128]{1,0:T(8,128)(2,1)} %get-tuple-element.40), channel_id=1, source_target_pairs={{0,8},{8,16},{16,24},{24,0},{1,9},{9,17},{17,25},{25,1},{2,10},{10... | collective-permute-start | bytes 1572872 | tf_op jit(solution)/shard_map/ppermute | solution.py:227
  574.3 74.8 %collective-permute-start.23 = (bf16[2048,128]{1,0:T(8,128)(2,1)}, bf16[2048,128]{1,0:T(8,128)(2,1)}, u32[]{:S(2)}, u32[]{:S(2)}) collective-permute-start(bf16[2048,128]{1,0:T(8,128)(2,1)} %get-tuple-element.52), channel_id=1, source_target_pairs={{0,8},{8,16},{16,24},{24,0},{1,9},{9,17},{17,25},{25,1},{2,10},{10... | collective-permute-start | bytes 1572872 | tf_op jit(solution)/shard_map/ppermute | solution.py:227
  631.8 63.9 %collective-permute-start.15 = (bf16[2048,128]{1,0:T(8,128)(2,1)S(1)}, bf16[2048,128]{1,0:T(8,128)(2,1)}, u32[]{:S(2)}, u32[]{:S(2)}) collective-permute-start(bf16[2048,128]{1,0:T(8,128)(2,1)S(1)} %copy-done.20), channel_id=1, source_target_pairs={{0,24},{8,0},{16,8},{24,16},{1,25},{9,1},{17,9},{25,17},{2,26},{10... | collective-permute-start | bytes 1572872 | tf_op jit(solution)/shard_map/ppermute | solution.py:227
  634.2 63.8 %collective-permute-start.16 = (bf16[2048,128]{1,0:T(8,128)(2,1)S(1)}, bf16[2048,128]{1,0:T(8,128)(2,1)}, u32[]{:S(2)}, u32[]{:S(2)}) collective-permute-start(bf16[2048,128]{1,0:T(8,128)(2,1)S(1)} %copy-done.14), channel_id=1, source_target_pairs={{0,16},{8,24},{16,0},{24,8},{1,17},{9,25},{17,1},{25,9},{2,18},{10... | collective-permute-start | bytes 1572872 | tf_op jit(solution)/shard_map/ppermute | solution.py:227
  640.5 59.8 %collective-permute-start.17 = (bf16[2048,128]{1,0:T(8,128)(2,1)S(1)}, bf16[2048,128]{1,0:T(8,128)(2,1)}, u32[]{:S(2)}, u32[]{:S(2)}) collective-permute-start(bf16[2048,128]{1,0:T(8,128)(2,1)S(1)} %copy-done.12), channel_id=1, source_target_pairs={{0,8},{8,16},{16,24},{24,0},{1,9},{9,17},{17,25},{25,1},{2,10},{10... | collective-permute-start | bytes 1572872 | tf_op jit(solution)/shard_map/ppermute | solution.py:227
  643.3 59.3 %collective-permute-start.21 = (bf16[2048,128]{1,0:T(8,128)(2,1)S(1)}, bf16[2048,128]{1,0:T(8,128)(2,1)}, u32[]{:S(2)}, u32[]{:S(2)}) collective-permute-start(bf16[2048,128]{1,0:T(8,128)(2,1)S(1)} %copy-done.10), channel_id=1, source_target_pairs={{0,24},{8,0},{16,8},{24,16},{1,25},{9,1},{17,9},{25,17},{2,26},{10... | collective-permute-start | bytes 1572872 | tf_op jit(solution)/shard_map/ppermute | solution.py:227
  649.0 70.0 %collective-permute-start.22 = (bf16[2048,128]{1,0:T(8,128)(2,1)S(1)}, bf16[2048,128]{1,0:T(8,128)(2,1)}, u32[]{:S(2)}, u32[]{:S(2)}) collective-permute-start(bf16[2048,128]{1,0:T(8,128)(2,1)S(1)} %copy-done.8), channel_id=1, source_target_pairs={{0,16},{8,24},{16,0},{24,8},{1,17},{9,25},{17,1},{25,9},{2,18},{10... | collective-permute-start | bytes 1572872 | tf_op jit(solution)/shard_map/ppermute | solution.py:227
  (79 other events, 1650.2 us)
Sparse Core Ops, SparseCore 0:
  27.6 36.7 all-reduce.2
  94.1 45.7 all-gather.6
  147.8 45.7 all-gather.8
